TPU v7x, 256 devices: a whole 4x4x8 slice. The times are simulated.
256 devices in a mesh: rep: 2 (over z_hi), ctx: 128 (over x, y, z_lo, core).
Axes of the slice: x: 4, y: 4, z: 8 (z_hi: 2, z_lo: 4; z = z_hi * 4 + z_lo), core: 2. Of those that a mesh axis runs over, the one named last changes fastest.
Arguments:
- inputs: bfloat16 [2, 16384, 4096], P('rep', 'ctx'), may hold values from -6 to 6
- gate_li: bfloat16 [2, 16384, 4096], P('rep', 'ctx'), may hold values from -6 to 6
- gate_mr: bfloat16 [2, 16384, 4096], P('rep', 'ctx'), may hold values from -6 to 6
- cotangent: bfloat16 [2, 16384, 4096], P('rep', 'ctx'), may hold values from -6 to 6
- residues: float32 [128, 16], replicated, may hold values from -1.5 to 1.5
- rates: float32 [128, 16], replicated, may hold values from 1.2207031e-05 to 0.05
- taps: float32 [128, 128], replicated, may hold values from -0.5 to 0.5
Outputs:
- grad_inputs: bfloat16 [2, 16384, 4096], P('rep', 'ctx')
- grad_gate_li: bfloat16 [2, 16384, 4096], P('rep', 'ctx')
- grad_gate_mr: bfloat16 [2, 16384, 4096], P('rep', 'ctx')
- grad_residues: float32 [128, 16], replicated
- grad_taps: float32 [128, 128], replicated
All inputs are finite; a program needn't handle non-finite values.
Results may differ from a plain program's by a relative error of at most 0.0049.
Values may be sent and summed in bfloat16 or wider, within the bound.
No kernel may reach another device: no remote copies, remote signals or barrier semaphores. Data moves between devices by JAX's collectives and lax.ppermute only.
A program may use at most 320 MiB of HBM per device.

v0:
```python
import math
import jax
import jax.numpy as jnp
from jax import lax
from jax.sharding import PartitionSpec as P


def from_behind(block, axis, distance):
    devices = range(lax.axis_size(axis))
    route = [(i - distance, i) for i in devices if i - distance in devices]
    return lax.ppermute(block, axis, route)


def contract(form, left_op, right_op):
    return jnp.einsum(form, left_op, right_op, precision=lax.Precision.HIGHEST)


def diagonal_matrix(diag_vals, rows, cols):
    lead = diag_vals.shape[:-1]
    period = rows + cols
    reverse_vals = jnp.flip(diag_vals, -1)
    padded = jnp.concatenate([reverse_vals, jnp.zeros(lead + (1,), reverse_vals.dtype)], axis=-1)
    tiled = jnp.tile(padded, (1,) * len(lead) + (rows + 1,))
    window = tiled[..., rows - 1 : rows - 1 + rows * (period - 1)]
    return window.reshape(lead + (rows, period - 1))[..., :cols]


def li_matrix(kernel):
    block_len = kernel.shape[-1]
    lead = kernel.shape[:-1]
    diag_vals = jnp.concatenate([jnp.zeros(lead + (block_len - 1,), kernel.dtype), kernel], axis=-1)
    return diagonal_matrix(diag_vals, block_len, block_len)


def mr_matrix(tap_rows):
    block_len = tap_rows.shape[-1]
    lead = tap_rows.shape[:-1]
    diag_vals = jnp.concatenate(
        [
            jnp.zeros(lead + (block_len - 1,), tap_rows.dtype),
            tap_rows,
            jnp.zeros(lead + (block_len,), tap_rows.dtype),
        ],
        axis=-1,
    )
    return diagonal_matrix(diag_vals, block_len, 2 * block_len)


def mode_tables(rates_part, residues_part, block_len):
    steps_up = jnp.arange(block_len).astype(jnp.float32)
    lam_rows = jnp.exp(-rates_part[:, :, None] * steps_up)
    norm_factor = jnp.sqrt(-jnp.expm1(-2.0 * rates_part))
    weight = residues_part * norm_factor
    kernel = contract("gm,gmk->gk", weight, lam_rows)
    toeplitz = li_matrix(kernel)
    end_powers = jnp.exp(-rates_part[:, :, None] * (block_len - 1.0 - steps_up))
    starts = jnp.exp(-rates_part[:, :, None] * (steps_up + 1.0))
    decay_rate = jnp.exp(-rates_part * block_len)
    return (toeplitz, lam_rows, end_powers, starts, decay_rate, norm_factor, weight, kernel)


def link_states(earlier, later_one):
    return (earlier[0] * later_one[0], later_one[0] * earlier[1] + later_one[1])


def nothing_before(total_a, total_b):
    return jnp.zeros_like(total_b)


def chain_states(decay_rate, block_ends, outside):
    nblocks = block_ends.shape[0]
    factor = jnp.broadcast_to(
        decay_rate.T[None, :, :, None], (nblocks,) + decay_rate.T.shape + (1,)
    )
    inc_a, inc_b = lax.associative_scan(link_states, (factor, block_ends), axis=0)
    before_a = jnp.concatenate([jnp.ones_like(inc_a[:1]), inc_a[:-1]], axis=0)
    before_b = jnp.concatenate([jnp.zeros_like(inc_b[:1]), inc_b[:-1]], axis=0)
    from_device = outside(inc_a[-1], inc_b[-1])
    return before_b + before_a * from_device[None]


def long_filter(seq_blocks, tables, outside):
    toeplitz, lam_rows, end_powers, starts, decay_rate, norm_factor, weight, kernel = tables
    local_part = contract("gtu,nugc->ntgc", toeplitz, seq_blocks)
    block_ends = contract("gmu,nugc->nmgc", end_powers, seq_blocks)
    entering = chain_states(decay_rate, block_ends, outside)
    carried = contract("gmt,nmgc->ntgc", starts * weight[:, :, None], entering)
    return (local_part + carried, entering)


def residue_grad(cot_blocks, seq_blocks, entering, tables):
    toeplitz, lam_rows, end_powers, starts, decay_rate, norm_factor, weight, kernel = tables
    cross_terms = contract("ntgc,nugc->gtu", cot_blocks, seq_blocks)
    unused_value, pull_back = jax.vjp(li_matrix, kernel)
    lag_totals = pull_back(cross_terms)[0]
    from_before = contract("gmt,ntgc->nmgc", starts, cot_blocks)
    first_part = jnp.sum(from_before * entering, axis=(0, 3)).T
    return norm_factor * (first_part + contract("gk,gmk->gm", lag_totals, lam_rows))


def make_pairs(extended, block_len):
    nblocks = extended.shape[0] // block_len - 1
    split_rows = extended.reshape((nblocks + 1, block_len) + extended.shape[1:])
    return jnp.concatenate([split_rows[:-1], split_rows[1:]], axis=1)


def on_device(inputs, gate_li, gate_mr, cotangent, residues, rates, taps):
    row_count = inputs.shape[1]
    width_all = inputs.shape[2]
    block_len = taps.shape[1]
    groups_all = residues.shape[0]
    group_size = width_all // groups_all
    blocks_dev = row_count // block_len
    gate_one = gate_li[0].astype(jnp.float32)
    gate_two = gate_mr[0].astype(jnp.float32)
    cot_out = cotangent[0].astype(jnp.float32)
    ctx_count = lax.axis_size("ctx")
    local_width = width_all // ctx_count
    members = min(group_size, local_width)
    owned_groups = local_width // members
    first_group = lax.axis_index("ctx") * local_width // group_size
    rates_part = lax.dynamic_slice_in_dim(rates, first_group, owned_groups, 0)
    residues_part = lax.dynamic_slice_in_dim(residues, first_group, owned_groups, 0)
    tables = mode_tables(rates_part, residues_part, block_len)
    spread = lax.all_to_all(inputs, "ctx", split_axis=2, concat_axis=1, tiled=True)
    seq_rows = spread.shape[1]
    seq_blocks = (
        spread[0]
        .astype(jnp.float32)
        .reshape(seq_rows // block_len, block_len, owned_groups, members)
    )
    values_ch, entering = long_filter(seq_blocks, tables, nothing_before)
    values = lax.all_to_all(
        values_ch.reshape(1, seq_rows, local_width), "ctx", split_axis=1, concat_axis=2, tiled=True
    )[0]
    mixer_in = (gate_one * values).astype(jnp.bfloat16)
    before = from_behind(mixer_in, "ctx", 1)
    extended = jnp.concatenate([before, mixer_in], axis=0)
    extended = extended.astype(jnp.float32).reshape(row_count + block_len, groups_all, group_size)
    in_pairs = make_pairs(extended, block_len)
    forward_taps = mr_matrix(taps)
    mixed_out = contract("gts,nsgc->ntgc", forward_taps, in_pairs).reshape(row_count, width_all)
    grad_gate_mr = (cot_out * mixed_out).astype(jnp.bfloat16)
    scaled = (cot_out * gate_two).astype(jnp.bfloat16)
    rows_after = from_behind(scaled, "ctx", -1)
    ext_cot = jnp.concatenate([scaled, rows_after], axis=0)
    ext_cot = ext_cot.astype(jnp.float32).reshape(row_count + block_len, groups_all, group_size)
    cot_pairs = jnp.flip(make_pairs(ext_cot, block_len), 1)
    grad_mixer = jnp.flip(contract("gts,nsgc->ntgc", forward_taps, cot_pairs), 1).reshape(
        row_count, width_all
    )
    scaled_blocks = scaled.astype(jnp.float32).reshape(
        blocks_dev, block_len, groups_all, group_size
    )
    cross_taps = contract("ntgc,nsgc->gts", scaled_blocks, in_pairs)
    unused_matrix, tap_pull = jax.vjp(mr_matrix, taps)
    grad_taps = tap_pull(cross_taps)[0]
    grad_gate_li = (grad_mixer * values).astype(jnp.bfloat16)
    cot_li = grad_mixer * gate_one
    cot_spread = lax.all_to_all(cot_li[None], "ctx", split_axis=2, concat_axis=1, tiled=True)[0]
    cot_blocks = cot_spread.reshape(seq_rows // block_len, block_len, owned_groups, members)
    flipped = jnp.flip(cot_blocks, (0, 1))
    back_blk, unused_states = long_filter(flipped, tables, nothing_before)
    back_ch = jnp.flip(back_blk, (0, 1)).reshape(1, seq_rows, local_width)
    grad_inputs = lax.all_to_all(
        back_ch.astype(jnp.bfloat16), "ctx", split_axis=1, concat_axis=2, tiled=True
    ).astype(back_ch.dtype)[0]
    part_res = residue_grad(cot_blocks, seq_blocks, entering, tables)
    grad_res = lax.dynamic_update_slice_in_dim(jnp.zeros_like(residues), part_res, first_group, 0)
    summed = lax.psum((grad_res, grad_taps), ("rep", "ctx"))
    grad_scale = 1.0 / math.sqrt(lax.axis_size("rep") * seq_rows)
    return (
        grad_inputs.astype(jnp.bfloat16)[None],
        grad_gate_li[None],
        grad_gate_mr[None],
        summed[0] * grad_scale,
        summed[1] * grad_scale,
    )


def solution(mesh):
    in_specs = (
        P("rep", "ctx", None),
        P("rep", "ctx", None),
        P("rep", "ctx", None),
        P("rep", "ctx", None),
        P(),
        P(),
        P(),
    )
    out_specs = (P("rep", "ctx", None), P("rep", "ctx", None), P("rep", "ctx", None), P(), P())
    return jax.shard_map(
        on_device, mesh=mesh, in_specs=in_specs, out_specs=out_specs, check_vma=False
    )
```

profile of v0, /device:TPU:1, one launch (start us, length us, event | category | flops | bytes accessed | tf_op | source)
XLA Modules:
  0.0 1296.1 jit_solution(12394947973667064074)
XLA Ops:
  7.2 5.0 copy.187
  12.7 22.3 %reduce.7 = bf16[4096,128]{1,0:T(8,128)(2,1)S(1)} reduce(bf16[4096,1,128]{2,1,0:T(2,128)(2,1)S(1)} %bitcast.245, bf16[]{:T(256)} %broadcast.484), dimensions={1}, to_apply=%bitcast.210.reduce_sub_computation | reduce | bytes 2097154
  36.2 14.1 %all-to-all-start.2 = ((bf16[128,2,2048]{2,1,0:T(2,128)(2,1)}), bf16[128,2,2048]{2,1,0:T(2,128)(2,1)S(1)}, u32[]{:S(2)}, u32[]{:S(2)}) async-start(bf16[128,2,2048]{2,1,0:T(2,128)(2,1)} %reshape.684), calls=%async_computation.2 | async-start | bytes 2097152 | tf_op jit(solution)/shard_map/all_to_all | solution.py:125
  56.7 23.0 %all-to-all-done.2 = bf16[128,2,2048]{2,1,0:T(2,128)(2,1)S(1)} async-done(((bf16[128,2,2048]{2,1,0:T(2,128)(2,1)}), bf16[128,2,2048]{2,1,0:T(2,128)(2,1)S(1)}, u32[]{:S(2)}, u32[]{:S(2)}) %all-to-all-start.2) | async-done | bytes 1048608 | tf_op jit(solution)/shard_map/all_to_all | solution.py:125
  88.0 22.4 %pad.354 = f32[128,16,1,32]{3,1,0,2:T(8,128)S(1)} pad(f32[64,16,1,32]{3,1,0,2:T(8,128)} %add.351, f32[]{:T(128)} %constant.15.clone.1), padding=1_0_1x0_0_0x0_0_0x0_0_0 | pad | bytes 393220
  114.4 2.4 fusion.9
  116.8 1.9 copy.192
  118.7 13.9 %copy.193 = f32[1,16384,32]{2,0,1:T(1,128)} copy(f32[1,16384,32]{1,0,2:T(1,128)S(1)} %bitcast.242) | data formatting | bytes 4194304 | tf_op jit(solution)/shard_map/reshape | solution.py:134
  133.1 74.7 %reduce.8 = f32[16384,32]{1,0:T(8,128)} reduce(f32[16384,1,32]{2,1,0:T(1,128)} %bitcast.224, f32[]{:T(128)} %broadcast.485), dimensions={1}, to_apply=%bitcast.212.reduce_sub_computation | reduce | bytes 4194308
  207.8 7.8 reshape.686
  215.6 8.0 all-to-all-start.3
  224.3 50.9 %all-to-all-done.3 = f32[128,1,4096]{2,1,0:T(1,128)} async-done(((f32[128,1,4096]{2,1,0:T(1,128)}), f32[128,1,4096]{2,1,0:T(1,128)}, u32[]{:S(2)}, u32[]{:S(2)}) %all-to-all-start.3) | async-done | bytes 2097184 | tf_op jit(solution)/shard_map/all_to_all | solution.py:133
  275.1 7.3 reduce.9
  282.5 15.5 %reshape.687 = f32[16384,1,32]{2,1,0:T(1,128)} reshape(f32[128,4096]{1,0:T(8,128)S(1)} %reduce.9) | data formatting | bytes 4194304
  297.9 19.4 %copy.194 = f32[1,16384,32]{1,0,2:T(1,128)} copy(f32[1,16384,32]{2,0,1:T(1,128)} %bitcast.225) | data formatting | bytes 4194304 | tf_op jit(solution)/shard_map/all_to_all | solution.py:133
  317.4 2.8 copy.195
  321.4 1.9 collective-permute-start.1
  324.5 11.5 tile.20
  336.0 17.0 %slice.430 = f32[128,49024]{0,1:T(8,128)} slice(f32[128,49536]{0,1:T(8,128)} %bitcast.223), slice={[0:128], [127:49151]} | slice | bytes 50200576 | tf_op jit(solution)/shard_map/slice | solution.py:24
  353.0 22.3 %reshape.679 = f32[128,128,383]{0,2,1:T(8,128)} reshape(f32[128,49024]{0,1:T(8,128)} %slice.430) | data formatting | bytes 50200576 | tf_op jit(solution)/shard_map/reshape | solution.py:25
  375.3 11.6 slice.431
  387.0 17.7 %copy.208 = f32[128,128,256]{2,1,0:T(8,128)} copy(f32[128,128,256]{0,2,1:T(8,128)} %slice.431) | data formatting | bytes 33554432
  404.7 2.3 copy.174
  406.9 2.3 copy.175
  411.3 21.5 %fusion.3 = f32[128,32,128]{2,1,0:T(8,128)S(1)} fusion(f32[128,128,256]{2,1,0:T(8,128)} %copy.208, f32[1,128,128,32]{1,3,2,0:T(8,128)S(1)} %bitcast.234, f32[1,128,128,32]{1,3,2,0:T(8,128)S(1)} %bitcast.232), kind=kOutput, calls=%fused_computation.5 | convolution fusion | flops 1611661312 | bytes 23068672 | tf_op jit(solution)/shard_map/gts,nsgc->ntgc/dot_general | solution.py:15
  434.2 3.4 collective-permute-start
  437.6 12.7 collective-permute-done
  450.9 2.5 pad_maximum_fusion
  453.4 7.4 rev.27
  460.8 22.1 %fusion.12 = f32[1,128,128,32]{1,3,2,0:T(8,128)} fusion(f32[128,128,256]{2,1,0:T(8,128)} %copy.208, f32[1,256,128,32]{1,3,2,0:T(8,128)} %rev.27), kind=kOutput, calls=%fused_computation.23 | convolution fusion | flops 1610612736 | bytes 23068672 | tf_op jit(solution)/shard_map/gts,nsgc->ntgc/dot_general | solution.py:15
  482.9 4.2 rev.29
  487.1 3.1 fusion.8
  490.2 67.2 %all_to_all.63 = f32[1,128,4096]{1,0,2:T(1,128)S(1)} all-to-all(f32[1,128,4096]{1,0,2:T(1,128)S(1)} %bitcast.246), channel_id=1, replica_groups=mesh['rep'=2,'ctx'=128] {'ctx'}, dimensions={2} | all-to-all | bytes 4194304 | tf_op jit(solution)/shard_map/all_to_all | solution.py:160
  557.3 2.3 rev.30
  559.7 9.8 convolution_bitcast_fusion.1
  579.0 3.2 pad.165
  582.2 3.2 pad.166
  588.5 2.8 pad.168
  592.8 4.7 pad.167
  600.2 8.5 pad.170
  612.2 15.1 %pad.172 = f32[64,16,1,32]{3,1,0,2:T(8,128)} pad(f32[32,16,1,32]{3,1,0,2:T(8,128)} %add.316, f32[]{:T(128)} %constant.15.clone.1), padding=1_0_1x0_0_0x0_0_0x0_0_0 | pad | bytes 196612 | tf_op jit(solution)/shard_map/pad | solution.py:75
  628.3 10.3 pad.171
  641.0 20.1 %pad.258 = f32[127,16,1,32]{3,1,0,2:T(8,128)} pad(f32[64,16,1,32]{3,1,0,2:T(8,128)S(1)} %pad_maximum_fusion.1, f32[]{:T(128)} %constant.15.clone.1), padding=0_0_1x0_0_0x0_0_0x0_0_0 | pad | bytes 391172 | tf_op jit(solution)/shard_map/slice | solution.py:77
  661.1 22.4 %pad.352 = f32[128,16,1,32]{3,1,0,2:T(8,128)S(1)} pad(f32[64,16,1,32]{3,1,0,2:T(8,128)} %add.318, f32[]{:T(128)} %constant.15.clone.1), padding=1_0_1x0_0_0x0_0_0x0_0_0 | pad | bytes 393220
  685.8 3.5 fusion.47
  689.2 3.3 add_bitcast_fusion
  692.6 11.4 rev.32
  705.5 12.8 copy.184
  718.3 91.1 %reduce.10 = bf16[16384,32]{1,0:T(8,128)(2,1)} reduce(bf16[16384,1,32]{2,1,0:T(2,128)(2,1)} %bitcast.226, bf16[]{:T(256)} %broadcast.484), dimensions={1}, to_apply=%bitcast.208.reduce_sub_computation | reduce | bytes 2097154
  809.4 7.3 reshape.682
  816.7 7.5 all-to-all-start.1
  824.3 8.8 fusion.2
  833.2 9.1 pad.205
  842.3 26.8 %reshape.667 = f32[128,49024]{1,0:T(8,128)} reshape(f32[128,128,383]{2,1,0:T(8,128)} %pad.205) | data formatting | bytes 50200576 | tf_op jit(solution)/shard_map/transpose(jvp())/reshape | solution.py:25
  869.1 24.7 %copy.212 = f32[128,49024]{0,1:T(8,128)} copy(f32[128,49024]{1,0:T(8,128)} %reshape.667) | data formatting | bytes 50200576
  893.8 19.2 %pad.206.clone = f32[128,49536]{0,1:T(8,128)} pad(f32[128,49024]{0,1:T(8,128)} %copy.212, f32[]{:T(128)} %constant.15.clone.1), padding=0_0x127_385 | pad | bytes 50462724 | tf_op jit(solution)/shard_map/transpose(jvp())/pad | solution.py:24
  913.0 9.3 reduce_sum.32
  922.9 2.4 copy.202
  925.3 236.1 %all-reduce.53.cloned.1.call-done = f32[128,128]{0,1:T(8,128)} async-done(((f32[128,128]{0,1:T(8,128)}), f32[128,128]{0,1:T(8,128)}) %all-reduce.53.cloned.1.call-update) | async-done | bytes 65552 | tf_op jit(solution)/shard_map/psum | solution.py:170
  1163.0 2.4 copy.201
  1168.3 9.6 fusion.18
  1178.3 74.4 %psum.14 = f32[128,16]{0,1:T(8,128)S(1)} all-reduce(f32[128,16]{0,1:T(8,128)S(1)} %dynamic_update_slice.3), channel_id=1, replica_groups=mesh['rep'=2,'ctx'=128] {'rep','ctx'}, use_global_device_ids=true, to_apply=%region_2.3 | all-reduce | flops 2048 | bytes 16384 | tf_op jit(solution)/shard_map/psum | solution.py:170
  1253.3 18.4 %reshape.683 = bf16[16384,1,32]{2,1,0:T(2,128)(2,1)} reshape(bf16[128,2,2048]{2,1,0:T(2,128)(2,1)} %all-to-all-done.1) | data formatting | bytes 2097152
  1271.7 15.1 %copy.185 = bf16[1,16384,32]{1,2,0:T(8,128)(2,1)S(1)} copy(bf16[1,16384,32]{2,0,1:T(2,128)(2,1)} %bitcast.227) | data formatting | bytes 2097152 | tf_op jit(solution)/shard_map/all_to_all | solution.py:165
  (273 shorter events, 62.9 us)
Async XLA Ops:
  35.0 15.3 %copy-start.32 = (f32[128,16]{0,1:T(8,128)S(1)}, f32[128,16]{0,1:T(8,128)}, u32[]{:S(2)}) copy-start(f32[128,16]{0,1:T(8,128)} %param.12) | copy-start | bytes 24580
  35.0 15.3 %copy-start.33 = (f32[128,16]{0,1:T(8,128)S(1)}, f32[128,16]{0,1:T(8,128)}, u32[]{:S(2)}) copy-start(f32[128,16]{0,1:T(8,128)} %param.11) | copy-start | bytes 24580
  36.2 43.5 %all-to-all-start.2 = ((bf16[128,2,2048]{2,1,0:T(2,128)(2,1)}), bf16[128,2,2048]{2,1,0:T(2,128)(2,1)S(1)}, u32[]{:S(2)}, u32[]{:S(2)}) async-start(bf16[128,2,2048]{2,1,0:T(2,128)(2,1)} %reshape.684), calls=%async_computation.2 | async-start | bytes 2097152 | tf_op jit(solution)/shard_map/all_to_all | solution.py:125
  50.5 4.1 copy-start.42
  50.5 519.0 %copy-start.20 = (f32[1,16]{1,0:T(1,128)}, f32[1,16]{1,0:T(1,128)S(1)}, u32[]{:S(2)}) copy-start(f32[1,16]{1,0:T(1,128)S(1)} %get-tuple-element.31) | copy-start | bytes 196
  50.5 32.5 %copy-start.36 = (f32[16]{0:T(128)}, f32[16]{0:T(128)S(1)}, u32[]{:S(2)}) copy-start(f32[16]{0:T(128)S(1)} %get-tuple-element.57) | copy-start | bytes 196
  50.5 32.6 %copy-start.30 = (f32[16]{0:T(128)}, f32[16]{0:T(128)S(1)}, u32[]{:S(2)}) copy-start(f32[16]{0:T(128)S(1)} %get-tuple-element.60) | copy-start | bytes 196
  50.5 32.7 %copy-start.28 = (f32[16]{0:T(128)}, f32[16]{0:T(128)S(1)}, u32[]{:S(2)}) copy-start(f32[16]{0:T(128)S(1)} %get-tuple-element.59) | copy-start | bytes 196
  50.6 32.9 %copy-start.26 = (f32[16]{0:T(128)}, f32[16]{0:T(128)S(1)}, u32[]{:S(2)}) copy-start(f32[16]{0:T(128)S(1)} %get-tuple-element.58) | copy-start | bytes 196
  50.6 519.1 %copy-start.22 = (f32[16]{0:T(128)}, f32[16]{0:T(128)S(1)}, u32[]{:S(2)}) copy-start(f32[16]{0:T(128)S(1)} %get-tuple-element.62) | copy-start | bytes 196
  50.6 520.0 %copy-start.25 = (f32[16]{0:T(128)}, f32[16]{0:T(128)S(1)}, u32[]{:S(2)}) copy-start(f32[16]{0:T(128)S(1)} %get-tuple-element.61) | copy-start | bytes 196
  54.3 26.5 %copy-start.44 = (f32[128]{0:T(128)}, f32[128]{0:T(128)S(1)}, u32[]{:S(2)}) copy-start(f32[128]{0:T(128)S(1)} %iota_convert_fusion) | copy-start | bytes 1540
  54.3 58.1 %copy-start.38 = (f32[16]{0:T(128)}, f32[16]{0:T(128)S(1)}, u32[]{:S(2)}) copy-start(f32[16]{0:T(128)S(1)} %get-tuple-element.48) | copy-start | bytes 196
  54.3 505.4 %copy-start.23 = (f32[16]{0:T(128)}, f32[16]{0:T(128)S(1)}, u32[]{:S(2)}) copy-start(f32[16]{0:T(128)S(1)} %get-tuple-element.49) | copy-start | bytes 196
  56.5 24.4 %copy-start.40 = (f32[128]{0:T(128)}, f32[128]{0:T(128)S(1)}, u32[]{:S(2)}) copy-start(f32[128]{0:T(128)S(1)} %broadcast_subtract_fusion) | copy-start | bytes 1540
  56.5 55.9 %copy-start.34 = (f32[128]{0:T(128)}, f32[128]{0:T(128)S(1)}, u32[]{:S(2)}) copy-start(f32[128]{0:T(128)S(1)} %broadcast_add_fusion) | copy-start | bytes 1540
  56.7 53.9 %copy-start.13 = (f32[128,16,1,1]{1,3,2,0:T(1,128)}, f32[128,16,1,1]{1,3,2,0:T(1,128)S(1)}, u32[]{:S(2)}) copy-start(f32[128,16,1,1]{1,3,2,0:T(1,128)S(1)} %pad_multiply_fusion) | copy-start | bytes 24580
  80.9 33.4 %copy-start.3 = (bf16[1,128,4096]{1,2,0:T(8,128)(2,1)}, bf16[1,128,4096]{1,2,0:T(8,128)(2,1)S(1)}, u32[]{:S(2)}) copy-start(bf16[1,128,4096]{1,2,0:T(8,128)(2,1)S(1)} %copy.207) | copy-start | bytes 3145732
  110.6 1.0 copy-start.7
  111.9 2.4 copy-start.16
  215.6 8.0 copy-start.15
  215.6 59.5 %all-to-all-start.3 = ((f32[128,1,4096]{2,1,0:T(1,128)}), f32[128,1,4096]{2,1,0:T(1,128)}, u32[]{:S(2)}, u32[]{:S(2)}) async-start(f32[128,1,4096]{2,1,0:T(1,128)} %reshape.686), calls=%async_computation.3 | async-start | bytes 4194304 | tf_op jit(solution)/shard_map/all_to_all | solution.py:133
  320.2 3.2 copy-start.19
  321.4 87.8 %collective-permute-start.1 = (bf16[128,4096]{0,1:T(8,128)(2,1)}, bf16[128,4096]{0,1:T(8,128)(2,1)}, u32[]{:S(2)}, u32[]{:S(2)}) collective-permute-start(bf16[128,4096]{0,1:T(8,128)(2,1)} %fusion.7), channel_id=1, source_target_pairs={{0,1},{1,2},{2,3},{3,4},{4,5},{5,6},{6,7},{7,8},{8,9},{9,10},{10,1... | collective-permute-start | bytes 3145736 | tf_op jit(solution)/shard_map/ppermute | solution.py:11
  411.3 21.5 %copy-start.1 = (f32[128,4096]{0,1:T(8,128)}, f32[128,4096]{0,1:T(8,128)S(1)}, u32[]{:S(2)}) copy-start(f32[128,4096]{0,1:T(8,128)S(1)} %get-tuple-element.32) | copy-start | bytes 6291460
  411.3 21.5 %copy-start.2 = (f32[128,4096]{0,1:T(8,128)}, f32[128,4096]{0,1:T(8,128)S(1)}, u32[]{:S(2)}) copy-start(f32[128,4096]{0,1:T(8,128)S(1)} %get-tuple-element.33) | copy-start | bytes 6291460
  411.3 21.5 %copy-start.10 = (bf16[1,128,4096]{1,2,0:T(8,128)(2,1)S(1)}, bf16[1,128,4096]{1,2,0:T(8,128)(2,1)}, u32[]{:S(2)}) copy-start(bf16[1,128,4096]{1,2,0:T(8,128)(2,1)} %copy.174) | copy-start | bytes 3145732
  411.3 21.5 %copy-start.11 = (bf16[1,128,4096]{1,2,0:T(8,128)(2,1)S(1)}, bf16[1,128,4096]{1,2,0:T(8,128)(2,1)}, u32[]{:S(2)}) copy-start(bf16[1,128,4096]{1,2,0:T(8,128)(2,1)} %copy.175) | copy-start | bytes 3145732
  434.2 16.1 %copy-start.5 = (bf16[1,128,4096]{1,2,0:T(8,128)(2,1)}, bf16[1,128,4096]{1,2,0:T(8,128)(2,1)S(1)}, u32[]{:S(2)}) copy-start(bf16[1,128,4096]{1,2,0:T(8,128)(2,1)S(1)} %get-tuple-element.39) | copy-start | bytes 3145732
  434.2 16.1 %collective-permute-start = (bf16[128,4096]{0,1:T(8,128)(2,1)S(1)}, bf16[128,4096]{0,1:T(8,128)(2,1)S(1)}, u32[]{:S(2)}, u32[]{:S(2)}) collective-permute-start(bf16[128,4096]{0,1:T(8,128)(2,1)S(1)} %bitcast.239), channel_id=1, source_target_pairs={{1,0},{2,1},{3,2},{4,3},{5,4},{6,5},{7,6},{8,7},{9,8},{10,9},{11,1... | collective-permute-start | bytes 3145736 | tf_op jit(solution)/shard_map/ppermute | solution.py:11
  557.3 2.4 copy-start.41
  569.5 1.2 copy-start.27
  569.5 1.2 copy-start.29
  569.5 1.3 copy-start.31
  569.6 1.4 copy-start.37
  569.7 0.8 copy-start.12
  570.8 0.9 copy-start.18
  598.4 28.9 %slice-start = ((f32[64,16,1,32]{3,1,0,2:T(8,128)}), f32[1,16,1,32]{3,1,0,2:T(8,128)S(1)}, s32[]{:S(2)}) async-start(f32[64,16,1,32]{3,1,0,2:T(8,128)} %copy-done.12), calls=%async_computation.5 | async-start | bytes 16384 | tf_op jit(solution)/shard_map/slice | solution.py:75
  600.1 38.5 %copy-start.21 = (f32[1,16]{1,0:T(1,128)S(1)}, f32[1,16]{1,0:T(1,128)}, u32[]{:S(2)}) copy-start(f32[1,16]{1,0:T(1,128)} %copy-done.20) | copy-start | bytes 196
  638.6 1.4 copy-start.8
  638.6 1.5 copy-start.9
  661.1 23.7 %copy-start.14 = (f32[128,16,1,1]{1,3,2,0:T(1,128)S(1)}, f32[128,16,1,1]{1,3,2,0:T(1,128)}, u32[]{:S(2)}) copy-start(f32[128,16,1,1]{1,3,2,0:T(1,128)} %copy-done.13) | copy-start | bytes 24580
  684.9 0.9 copy-start.24
  684.9 0.9 copy-start.35
  684.9 0.9 copy-start.39
  685.7 3.5 copy-start
  685.7 3.5 copy-start.17
  816.7 7.6 copy-start.6
  816.7 436.6 %all-to-all-start.1 = ((bf16[128,2,2048]{2,1,0:T(2,128)(2,1)}), bf16[128,2,2048]{2,1,0:T(2,128)(2,1)}, u32[]{:S(2)}, u32[]{:S(2)}) async-start(bf16[128,2,2048]{2,1,0:T(2,128)(2,1)} %reshape.682), calls=%async_computation.1 | async-start | bytes 2097152 | tf_op jit(solution)/shard_map/all_to_all | solution.py:165
  824.2 337.1 %all-reduce.53.cloned.1.call-start = ((), (), s32[]{:S(2)}) async-start(), calls=%async_computation.4 | async-start | bytes 131072 | tf_op jit(solution)/shard_map/psum | solution.py:170
  922.9 242.5 %copy-start.4 = (bf16[1,128,4096]{1,2,0:T(8,128)(2,1)S(1)}, bf16[1,128,4096]{1,2,0:T(8,128)(2,1)}, u32[]{:S(2)}) copy-start(bf16[1,128,4096]{1,2,0:T(8,128)(2,1)} %copy-done.3) | copy-start | bytes 3145732
  1167.3 10.6 copy-start.43
  1167.3 10.6 copy-start.45
Sparse Core Ops, SparseCore 0:
  923.1 238.2 all-reduce.52
where the time goes:
time: 1310 us; the launch traced here: 1300 us
  local copies, waits for them, and re-layouts  453 us (35%)
  waiting for transfers between devices  323 us (25%)
  other arithmetic  243 us (19%)
  blocking collectives  142 us (11%)
  matrix products  86.1 us (7%)
  starting transfers between devices  35 us (3%)
  between operations  15.5 us (1%)
    psum x1, waiting for transfers between devices, on_device(): summed = lax.psum((grad_res, grad_taps), ('rep', 'ctx'))  236 us
    unnamed x3, other arithmetic  188 us
    unnamed x124, local copies, waits for them, and re-layouts  161 us
    dot_general x13, matrix products, contract(): return jnp.einsum(form, left_op, right_op, precision=lax.Precision.HIGHEST)  86.1 us
    psum x1, blocking collectives, on_device(): summed = lax.psum((grad_res, grad_taps), ('rep', 'ctx'))  74.4 us
    all_to_all x1, blocking collectives, on_device(): lax.all_to_all(cot_li[None], 'ctx', split_axis=2, concat_axis=1, tiled=True)  67.2 us
    pad x30, local copies, waits for them, and re-layouts, chain_states(): lax.associative_scan(link_states, (factor, block_ends), axis=0)  53 us
    all_to_all x1, waiting for transfers between devices, on_device(): lax.all_to_all(values_ch.reshape(1, seq_rows, local_width), 'ctx', split_...  50.9 us
  transfers between devices with their start and end apart: 6, of which 4 were waited for; matrix products, arithmetic and copies ran while one was open for 16% of the time, Pallas kernels for 0%

commit v1 on v0

--- a/solution.py
+++ b/solution.py
@@ -167,7 +167,7 @@
     ).astype(back_ch.dtype)[0]
     part_res = residue_grad(cot_blocks, seq_blocks, entering, tables)
     grad_res = lax.dynamic_update_slice_in_dim(jnp.zeros_like(residues), part_res, first_group, 0)
-    summed = lax.psum((grad_res, grad_taps), ("rep", "ctx"))
+    summed = lax.psum(lax.psum((grad_res, grad_taps), "ctx"), "rep")
     grad_scale = 1.0 / math.sqrt(lax.axis_size("rep") * seq_rows)
     return (
         grad_inputs.astype(jnp.bfloat16)[None],

time: 1310 us -> 2530 us (1.93)
  waiting for transfers between devices: 323 us -> 1260 us
  blocking collectives: 142 us -> 413 us
    psum x1 -> x2, waiting for transfers between devices: 236 us -> 1180 us  [on_device(): summed = lax.psum(lax.psum((grad_res, grad_taps), 'ctx'), 'rep')]
    psum x1 -> x2, blocking collectives: 74.4 us -> 345 us  [on_device(): summed = lax.psum(lax.psum((grad_res, grad_taps), 'ctx'), 'rep')]
  transfers between devices with their start and end apart: 6 -> 7, of which waited for: 4 -> 5; matrix products, arithmetic and copies ran while one was open for 16% -> 8% of each run, Pallas kernels for 0% -> 0%
where the time goes in v1:
time: 2530 us; the launch traced here: 2510 us
  waiting for transfers between devices  1260 us (50%)
  local copies, waits for them, and re-layouts  452 us (18%)
  blocking collectives  413 us (16%)
  other arithmetic  243 us (10%)
  matrix products  86.1 us (3%)
  starting transfers between devices  35 us (1%)
    psum x2, waiting for transfers between devices, on_device(): summed = lax.psum(lax.psum((grad_res, grad_taps), 'ctx'), 'rep')  1180 us
    psum x2, blocking collectives, on_device(): summed = lax.psum(lax.psum((grad_res, grad_taps), 'ctx'), 'rep')  345 us
    unnamed x3, other arithmetic  188 us
    unnamed x124, local copies, waits for them, and re-layouts  161 us
    dot_general x13, matrix products, contract(): return jnp.einsum(form, left_op, right_op, precision=lax.Precision.HIGHEST)  86.1 us
    all_to_all x1, blocking collectives, on_device(): lax.all_to_all(cot_li[None], 'ctx', split_axis=2, concat_axis=1, tiled=True)  67.2 us
    pad x30, local copies, waits for them, and re-layouts, chain_states(): lax.associative_scan(link_states, (factor, block_ends), axis=0)  53 us
    all_to_all x1, waiting for transfers between devices, on_device(): lax.all_to_all(values_ch.reshape(1, seq_rows, local_width), 'ctx', split_...  50.9 us
  transfers between devices with their start and end apart: 7, of which 5 were waited for; matrix products, arithmetic and copies ran while one was open for 8% of the time, Pallas kernels for 0%

profile of v1, /device:TPU:1, one launch (start us, length us, event | category | flops | bytes accessed | tf_op | source)
XLA Modules:
  0.0 2507.6 jit_solution(17987881698083840305)
XLA Ops:
  7.2 5.0 copy.187
  12.7 22.4 reduce.7
  36.2 14.1 all-to-all-start.2
  56.7 23.0 all-to-all-done.2
  88.1 22.4 pad.354
  114.4 2.4 fusion.9
  118.8 13.8 copy.193
  133.1 74.7 %reduce.8 = f32[16384,32]{1,0:T(8,128)} reduce(f32[16384,1,32]{2,1,0:T(1,128)} %bitcast.224, f32[]{:T(128)} %broadcast.485), dimensions={1}, to_apply=%bitcast.212.reduce_sub_computation | reduce | bytes 4194308
  207.8 7.8 reshape.686
  215.6 8.0 all-to-all-start.3
  224.3 50.9 %all-to-all-done.3 = f32[128,1,4096]{2,1,0:T(1,128)} async-done(((f32[128,1,4096]{2,1,0:T(1,128)}), f32[128,1,4096]{2,1,0:T(1,128)}, u32[]{:S(2)}, u32[]{:S(2)}) %all-to-all-start.3) | async-done | bytes 2097184 | tf_op jit(solution)/shard_map/all_to_all | solution.py:133
  275.2 7.3 reduce.9
  282.5 15.5 reshape.687
  298.0 19.5 copy.194
  317.4 2.8 copy.195
  324.6 11.5 tile.20
  336.1 17.0 slice.430
  353.1 22.3 reshape.679
  375.4 11.6 slice.431
  387.0 17.6 copy.208
  404.7 2.3 copy.174
  406.9 2.3 copy.175
  411.3 21.5 fusion.3
  434.2 3.4 collective-permute-start
  437.6 12.7 collective-permute-done
  450.9 2.5 pad_maximum_fusion
  453.4 7.4 rev.27
  460.8 22.1 fusion.12
  482.9 4.2 rev.29
  487.0 3.1 fusion.8
  490.1 67.2 %all_to_all.63 = f32[1,128,4096]{1,0,2:T(1,128)S(1)} all-to-all(f32[1,128,4096]{1,0,2:T(1,128)S(1)} %bitcast.246), channel_id=1, replica_groups=mesh['rep'=2,'ctx'=128] {'ctx'}, dimensions={2} | all-to-all | bytes 4194304 | tf_op jit(solution)/shard_map/all_to_all | solution.py:160
  557.3 2.3 rev.30
  559.6 9.8 convolution_bitcast_fusion.1
  578.9 3.2 pad.165
  582.2 3.2 pad.166
  588.4 2.8 pad.168
  592.7 4.7 pad.167
  600.1 8.5 pad.170
  612.1 15.1 pad.172
  628.2 10.3 pad.171
  641.0 20.1 pad.258
  661.1 22.4 pad.352
  685.7 3.5 fusion.47
  689.2 3.3 add_bitcast_fusion
  692.5 11.4 rev.32
  705.4 12.8 copy.184
  718.2 91.2 %reduce.10 = bf16[16384,32]{1,0:T(8,128)(2,1)} reduce(bf16[16384,1,32]{2,1,0:T(2,128)(2,1)} %bitcast.226, bf16[]{:T(256)} %broadcast.484), dimensions={1}, to_apply=%bitcast.208.reduce_sub_computation | reduce | bytes 2097154
  809.4 7.3 reshape.682
  816.7 7.5 all-to-all-start.1
  824.3 8.8 fusion.2
  833.1 9.0 pad.205
  842.1 26.8 %reshape.667 = f32[128,49024]{1,0:T(8,128)} reshape(f32[128,128,383]{2,1,0:T(8,128)} %pad.205) | data formatting | bytes 50200576 | tf_op jit(solution)/shard_map/transpose(jvp())/reshape | solution.py:25
  868.9 24.7 copy.212
  893.6 19.2 pad.206.clone
  912.8 9.3 reduce_sum.32
  922.8 1141.1 %all-reduce.54.cloned.1.call-done = f32[128,128]{0,1:T(8,128)} async-done(((f32[128,128]{0,1:T(8,128)}), f32[128,128]{0,1:T(8,128)}) %all-reduce.54.cloned.1.call-update) | async-done | bytes 65552 | tf_op jit(solution)/shard_map/psum | solution.py:170
  2063.9 2.6 copy.202
  2066.4 35.8 %all-reduce.56.cloned.1.call-done = f32[128,128]{0,1:T(8,128)} async-done(((f32[128,128]{0,1:T(8,128)}), f32[128,128]{0,1:T(8,128)}) %all-reduce.56.cloned.1.call-update) | async-done | bytes 65552 | tf_op jit(solution)/shard_map/psum | solution.py:170
  2103.8 2.3 copy.201
  2109.0 9.6 fusion.18
  2118.9 337.6 %psum.28 = f32[128,16]{0,1:T(8,128)S(1)} all-reduce(f32[128,16]{0,1:T(8,128)S(1)} %dynamic_update_slice.3), channel_id=1, replica_groups=mesh['rep'=2,'ctx'=128] {'ctx'}, use_global_device_ids=true, to_apply=%region_2.3 | all-reduce | flops 2048 | bytes 16384 | tf_op jit(solution)/shard_map/psum | solution.py:170
  2456.5 7.8 psum.29
  2464.9 18.3 reshape.683
  2483.2 15.1 copy.185
  (277 shorter events, 66.8 us)
Async XLA Ops:
  35.1 15.3 copy-start.32
  35.1 15.3 copy-start.33
  36.2 43.5 %all-to-all-start.2 = ((bf16[128,2,2048]{2,1,0:T(2,128)(2,1)}), bf16[128,2,2048]{2,1,0:T(2,128)(2,1)S(1)}, u32[]{:S(2)}, u32[]{:S(2)}) async-start(bf16[128,2,2048]{2,1,0:T(2,128)(2,1)} %reshape.684), calls=%async_computation.2 | async-start | bytes 2097152 | tf_op jit(solution)/shard_map/all_to_all | solution.py:125
  50.6 4.1 copy-start.42
  50.6 518.9 %copy-start.20 = (f32[1,16]{1,0:T(1,128)}, f32[1,16]{1,0:T(1,128)S(1)}, u32[]{:S(2)}) copy-start(f32[1,16]{1,0:T(1,128)S(1)} %get-tuple-element.31) | copy-start | bytes 196
  50.6 32.5 %copy-start.36 = (f32[16]{0:T(128)}, f32[16]{0:T(128)S(1)}, u32[]{:S(2)}) copy-start(f32[16]{0:T(128)S(1)} %get-tuple-element.57) | copy-start | bytes 196
  50.6 32.6 %copy-start.30 = (f32[16]{0:T(128)}, f32[16]{0:T(128)S(1)}, u32[]{:S(2)}) copy-start(f32[16]{0:T(128)S(1)} %get-tuple-element.60) | copy-start | bytes 196
  50.6 32.7 %copy-start.28 = (f32[16]{0:T(128)}, f32[16]{0:T(128)S(1)}, u32[]{:S(2)}) copy-start(f32[16]{0:T(128)S(1)} %get-tuple-element.59) | copy-start | bytes 196
  50.6 32.9 %copy-start.26 = (f32[16]{0:T(128)}, f32[16]{0:T(128)S(1)}, u32[]{:S(2)}) copy-start(f32[16]{0:T(128)S(1)} %get-tuple-element.58) | copy-start | bytes 196
  50.6 519.0 %copy-start.22 = (f32[16]{0:T(128)}, f32[16]{0:T(128)S(1)}, u32[]{:S(2)}) copy-start(f32[16]{0:T(128)S(1)} %get-tuple-element.62) | copy-start | bytes 196
  50.6 519.9 %copy-start.25 = (f32[16]{0:T(128)}, f32[16]{0:T(128)S(1)}, u32[]{:S(2)}) copy-start(f32[16]{0:T(128)S(1)} %get-tuple-element.61) | copy-start | bytes 196
  54.3 26.5 %copy-start.44 = (f32[128]{0:T(128)}, f32[128]{0:T(128)S(1)}, u32[]{:S(2)}) copy-start(f32[128]{0:T(128)S(1)} %iota_convert_fusion) | copy-start | bytes 1540
  54.4 58.1 %copy-start.38 = (f32[16]{0:T(128)}, f32[16]{0:T(128)S(1)}, u32[]{:S(2)}) copy-start(f32[16]{0:T(128)S(1)} %get-tuple-element.48) | copy-start | bytes 196
  54.4 505.3 %copy-start.23 = (f32[16]{0:T(128)}, f32[16]{0:T(128)S(1)}, u32[]{:S(2)}) copy-start(f32[16]{0:T(128)S(1)} %get-tuple-element.49) | copy-start | bytes 196
  56.5 24.4 copy-start.40
  56.5 56.0 %copy-start.34 = (f32[128]{0:T(128)}, f32[128]{0:T(128)S(1)}, u32[]{:S(2)}) copy-start(f32[128]{0:T(128)S(1)} %broadcast_add_fusion) | copy-start | bytes 1540
  56.7 53.9 %copy-start.13 = (f32[128,16,1,1]{1,3,2,0:T(1,128)}, f32[128,16,1,1]{1,3,2,0:T(1,128)S(1)}, u32[]{:S(2)}) copy-start(f32[128,16,1,1]{1,3,2,0:T(1,128)S(1)} %pad_multiply_fusion) | copy-start | bytes 24580
  81.0 33.5 %copy-start.3 = (bf16[1,128,4096]{1,2,0:T(8,128)(2,1)}, bf16[1,128,4096]{1,2,0:T(8,128)(2,1)S(1)}, u32[]{:S(2)}) copy-start(bf16[1,128,4096]{1,2,0:T(8,128)(2,1)S(1)} %copy.207) | copy-start | bytes 3145732
  110.6 1.0 copy-start.7
  112.0 2.4 copy-start.16
  215.6 8.0 copy-start.15
  215.6 59.5 %all-to-all-start.3 = ((f32[128,1,4096]{2,1,0:T(1,128)}), f32[128,1,4096]{2,1,0:T(1,128)}, u32[]{:S(2)}, u32[]{:S(2)}) async-start(f32[128,1,4096]{2,1,0:T(1,128)} %reshape.686), calls=%async_computation.3 | async-start | bytes 4194304 | tf_op jit(solution)/shard_map/all_to_all | solution.py:133
  320.2 3.2 copy-start.19
  321.4 87.7 %collective-permute-start.1 = (bf16[128,4096]{0,1:T(8,128)(2,1)}, bf16[128,4096]{0,1:T(8,128)(2,1)}, u32[]{:S(2)}, u32[]{:S(2)}) collective-permute-start(bf16[128,4096]{0,1:T(8,128)(2,1)} %fusion.7), channel_id=1, source_target_pairs={{0,1},{1,2},{2,3},{3,4},{4,5},{5,6},{6,7},{7,8},{8,9},{9,10},{10,1... | collective-permute-start | bytes 3145736 | tf_op jit(solution)/shard_map/ppermute | solution.py:11
  411.3 21.5 copy-start.1
  411.3 21.5 copy-start.2
  411.3 21.5 copy-start.10
  411.3 21.5 copy-start.11
  434.2 16.1 copy-start.5
  434.2 16.1 collective-permute-start
  557.3 2.3 copy-start.41
  569.5 1.2 copy-start.27
  569.5 1.2 copy-start.29
  569.5 1.3 copy-start.31
  569.5 1.4 copy-start.37
  569.7 0.8 copy-start.12
  570.7 0.9 copy-start.18
  598.4 28.9 %slice-start = ((f32[64,16,1,32]{3,1,0,2:T(8,128)}), f32[1,16,1,32]{3,1,0,2:T(8,128)S(1)}, s32[]{:S(2)}) async-start(f32[64,16,1,32]{3,1,0,2:T(8,128)} %copy-done.12), calls=%async_computation.6 | async-start | bytes 16384 | tf_op jit(solution)/shard_map/slice | solution.py:75
  600.1 38.5 %copy-start.21 = (f32[1,16]{1,0:T(1,128)S(1)}, f32[1,16]{1,0:T(1,128)}, u32[]{:S(2)}) copy-start(f32[1,16]{1,0:T(1,128)} %copy-done.20) | copy-start | bytes 196
  638.6 1.4 copy-start.8
  638.6 1.5 copy-start.9
  661.1 23.7 copy-start.14
  684.8 0.9 copy-start.24
  684.8 0.9 copy-start.35
  684.8 0.9 copy-start.39
  685.7 3.5 copy-start
  685.7 3.5 copy-start.17
  816.7 7.6 copy-start.6
  816.7 1648.2 %all-to-all-start.1 = ((bf16[128,2,2048]{2,1,0:T(2,128)(2,1)}), bf16[128,2,2048]{2,1,0:T(2,128)(2,1)}, u32[]{:S(2)}, u32[]{:S(2)}) async-start(bf16[128,2,2048]{2,1,0:T(2,128)(2,1)} %reshape.682), calls=%async_computation.1 | async-start | bytes 2097152 | tf_op jit(solution)/shard_map/all_to_all | solution.py:165
  824.2 1239.6 %all-reduce.54.cloned.1.call-start = ((), (), s32[]{:S(2)}) async-start(), calls=%async_computation.4 | async-start | bytes 131072 | tf_op jit(solution)/shard_map/psum | solution.py:170
  922.7 1179.5 %all-reduce.56.cloned.1.call-start = ((), (), s32[]{:S(2)}) async-start(), calls=%async_computation.5 | async-start | bytes 131072 | tf_op jit(solution)/shard_map/psum | solution.py:170
  2063.9 42.2 %copy-start.4 = (bf16[1,128,4096]{1,2,0:T(8,128)(2,1)S(1)}, bf16[1,128,4096]{1,2,0:T(8,128)(2,1)}, u32[]{:S(2)}) copy-start(bf16[1,128,4096]{1,2,0:T(8,128)(2,1)} %copy-done.3) | copy-start | bytes 3145732
  2107.9 10.6 copy-start.43
  2107.9 10.6 copy-start.45
Sparse Core Ops, SparseCore 0:
  922.8 1140.9 all-reduce.53
  2066.5 35.6 all-reduce.55
